TPU v7x, 32 devices: a whole 2x2x4 slice. The times are simulated.
32 devices in a mesh: grp: 4 (over z), dev: 8 (over y, x, core).
Axes of the slice: x: 2, y: 2, z: 4, core: 2. Of those that a mesh axis runs over, the one named last changes fastest.
Arguments:
- stored_tiles: float32 [32, 9, 128, 128], P(('grp', 'dev')), may hold values from -0.22097087 to 0.22097087, as said below
- tile_flags: int32 [32, 9], P(('grp', 'dev')), may hold values from 0 to 1, as said below
- orbitals: float32 [4096, 256], P(('grp', 'dev')), may hold values from -6 to 6
Outputs:
- product: float32 [4096, 256], P(('grp', 'dev'))
Inputs may be any that keep to these rules, and one draw needn't show every extreme that they name: tile_flags[p, s] is 1 at s = p mod 8, 0 for s below that, and 0 at s = 8 in the last 8 block rows. `stored_tiles`: the tile at slot p mod 8 of block row p is symmetric.
All inputs are finite; a program needn't handle non-finite values.
Results may differ from a plain program's by a relative error of at most 0.000075.
Values sent between devices are 32-bit elements; how exact they have to be, the bound alone decides.
No kernel may reach another device: no remote copies, remote signals or barrier semaphores. Data moves between devices by JAX's collectives and lax.ppermute only.
A program may use at most 64 MiB of HBM per device.

v0:
```python
import functools

import jax
import jax.numpy as jnp
from jax import lax
from jax.experimental import pallas as pl
from jax.experimental.pallas import tpu as pltpu
from jax.sharding import PartitionSpec as P

HBM = pl.BlockSpec(memory_space=pltpu.HBM)
VMEM = pl.BlockSpec(memory_space=pltpu.VMEM)
F32 = jnp.float32


def parted(value):
    high = value.astype(jnp.bfloat16)
    return high, (value - high.astype(F32)).astype(jnp.bfloat16)


def times(left, right):
    left_high, left_low = parted(left)
    right_high, right_low = parted(right)
    dot = functools.partial(jnp.dot, preferred_element_type=F32)
    rows = left.shape[0]
    both = dot(jnp.concatenate([left_high, left_low], axis=0), right_high)
    return both[:rows] + both[rows:] + dot(left_high, right_low)


def transposed_times(left, right):
    return times(left.T, right)


class Layout:
    def __init__(self, group_width):
        self.width = group_width
        self.pairs = group_width // 2
        self.rounds = (self.pairs - 1) // 2
        self.last_offset = 2

    def offset(self, round_index, side):
        if round_index == 0:
            return 1 + 2 * side
        return 2 * round_index + 2 + side


def place():
    index = lax.axis_index("dev")
    return index, index // 2, index % 2


def load_kernel(layout, flags_in, tiles_in, orbitals_in, tiles, orbitals, flags, sems):
    copies = [
        pltpu.make_async_copy(flags_in, flags, sems.at[0]),
        pltpu.make_async_copy(tiles_in, tiles, sems.at[1]),
        pltpu.make_async_copy(orbitals_in, orbitals, sems.at[2]),
    ]
    for copy in copies:
        copy.start()
    for copy in copies:
        copy.wait()
    for slot in range(layout.width + 1):
        tiles[slot] = tiles[slot] * flags[0, slot].astype(F32)


def mask_kernel(layout, flags, mask):
    row = flags[...].astype(F32)
    for slot in range(layout.width + 1):
        mask[slot : slot + 1] = jnp.broadcast_to(
            row[:, slot : slot + 1], (1, mask.shape[1])
        )


def taken_tile(taken, mask, slot):
    return taken[slot] * mask[pl.ds(slot, 1), :]


def pair_terms(far, tiles, taken, mask, own, other, out):
    lefts = []
    for k in range(2):
        slot = 2 * far + k
        stack = jnp.concatenate([tiles[slot], taken_tile(taken, mask, slot)], axis=0)
        lefts.append(stack.T)
    terms = times(
        jnp.concatenate(lefts, axis=0), jnp.concatenate([own, other], axis=0)
    )
    order = own.shape[0]
    out[0] = terms[:order]
    out[1] = terms[order:]


def send_full_kernel(layout, tiles, taken, mask, orbitals, taken_orbitals, *outs):
    index, pair, side = place()
    own, other = orbitals[...], taken_orbitals[...]
    for r in range(layout.rounds):
        far = pair ^ layout.offset(r, side)
        out = outs[r]

        @pl.when(far > pair)
        def _():
            pair_terms(far, tiles, taken, mask, own, other, out)

        @pl.when(far < pair)
        def _():
            out[0] = jnp.where(side == 0, own, other)
            out[1] = jnp.where(side == 0, other, own)

    far = pair ^ layout.last_offset

    @pl.when((side == 1) & (pair == 0))
    def _():
        pair_terms(far, tiles, taken, mask, own, other, outs[-1])


def send_last_kernel(layout, tiles, taken, mask, orbitals, taken_orbitals, made, out):
    index, pair, side = place()
    own, other = orbitals[...], taken_orbitals[...]
    far = pair ^ layout.last_offset
    lower = lax.axis_index("grp") % 2 == 0

    @pl.when((side == 1) & (pair == 0))
    def _():
        out[...] = made[...]

    @pl.when((side == 1) & (far > pair) & (pair > 0))
    def _():
        pair_terms(far, tiles, taken, mask, own, other, out)

    @pl.when((side == 1) & (far < pair))
    def _():
        out[0] = other
        out[1] = own

    @pl.when((side == 0) & lower)
    def _():
        out[0] = transposed_times(tiles[layout.width], own)
        out[1] = transposed_times(taken_tile(taken, mask, layout.width), other)

    @pl.when((side == 0) & jnp.logical_not(lower))
    def _():
        out[0] = own
        out[1] = other


def send_odd_kernel(layout, tiles, orbitals, out):
    lower = lax.axis_index("grp") % 2 == 1

    @pl.when(lower)
    def _():
        out[...] = transposed_times(tiles[layout.width], orbitals[...])

    @pl.when(jnp.logical_not(lower))
    def _():
        out[...] = orbitals[...]


def near_kernel(layout, tiles, orbitals, taken_orbitals, mine, others):
    index, pair, side = place()
    own, other = orbitals[...], taken_orbitals[...]
    beside = tiles[index ^ 1]
    row = jnp.concatenate([tiles[index], beside], axis=1)
    mine[...] = times(row, jnp.concatenate([own, other], axis=0))
    others[...] = transposed_times(beside, own)


def take_full(layout, arrived, row, tile_of, total):
    index, pair, side = place()
    for r, came in enumerate(arrived):
        far = pair ^ layout.offset(r, side)

        @pl.when(far > pair)
        def _():
            left = jnp.concatenate([tile_of(2 * far), tile_of(2 * far + 1)], axis=1)
            right = jnp.concatenate([came[0], came[1]], axis=0)
            total[...] += times(left, right)

        @pl.when(far < pair)
        def _():
            total[...] += came[side ^ row]


def full_kernel(layout, taken, mask, others_in, *refs):
    arrived, others = refs[:-1], refs[-1]
    others[...] = others_in[...]
    take_full(layout, arrived, 1, lambda slot: taken_tile(taken, mask, slot), others)


def back_kernel(layout, taken, mask, others_in, came, others):
    index, pair, side = place()
    far = pair ^ layout.last_offset
    lower = lax.axis_index("grp") % 2 == 0

    @pl.when((side == 1) & (far > pair))
    def _():
        left = jnp.concatenate(
            [taken_tile(taken, mask, 2 * far + k) for k in range(2)], axis=1
        )
        right = jnp.concatenate([came[0], came[1]], axis=0)
        others[...] = others_in[...] + times(left, right)

    @pl.when((side == 1) & (far < pair))
    def _():
        others[...] = others_in[...] + came[0]

    @pl.when((side == 0) & lower)
    def _():
        left = taken_tile(taken, mask, layout.width)
        others[...] = others_in[...] + times(left, came[1])

    @pl.when((side == 0) & jnp.logical_not(lower))
    def _():
        others[...] = others_in[...] + came[1]


def mine_kernel(layout, tiles, mine_in, came, odd_in, *refs):
    arrived, mine = refs[:-1], refs[-1]
    index, pair, side = place()
    far = pair ^ layout.last_offset
    group = lax.axis_index("grp")
    lower = group % 2 == 0

    @pl.when((side == 1) & (far > pair))
    def _():
        left = jnp.concatenate([tiles[2 * far], tiles[2 * far + 1]], axis=1)
        right = jnp.concatenate([came[0], came[1]], axis=0)
        mine[...] = mine_in[...] + times(left, right)

    @pl.when((side == 1) & (far < pair))
    def _():
        mine[...] = mine_in[...] + came[1]

    @pl.when((side == 0) & lower)
    def _():
        mine[...] = mine_in[...] + times(tiles[layout.width], came[0])

    @pl.when((side == 0) & jnp.logical_not(lower))
    def _():
        mine[...] = mine_in[...] + came[0]

    @pl.when(lower)
    def _():
        mine[...] += jnp.where(group > 0, odd_in[...], 0.0)

    @pl.when(jnp.logical_not(lower))
    def _():
        mine[...] += times(tiles[layout.width], odd_in[...])

    take_full(layout, arrived, 0, lambda slot: tiles[slot], mine)


def call(body, outs, operands, specs=None, scratch=(), flops=0):
    return pl.pallas_call(
        body,
        out_shape=outs,
        in_specs=specs or [VMEM] * len(operands),
        out_specs=jax.tree.map(lambda _: VMEM, outs),
        scratch_shapes=scratch,
        cost_estimate=pl.CostEstimate(
            flops=flops, bytes_accessed=0, transcendentals=0
        ),
        compiler_params=pltpu.CompilerParams(vmem_limit_bytes=32 * 1024 * 1024),
    )(*operands)


def last_moves(layout, groups):
    moves = []
    for g in range(groups):
        for i in range(layout.width):
            if i % 2 == 1:
                to, j = g, i ^ (2 * layout.last_offset)
            else:
                to, j = g ^ 1, i
                if to >= groups:
                    to = g
            moves.append((g * layout.width + i, to * layout.width + j))
    return moves


def odd_moves(layout, groups):
    moves = []
    for g in range(groups):
        to = g + 1 if g % 2 == 1 else g - 1
        for i in range(layout.width):
            if 0 <= to < groups:
                moves.append((g * layout.width + i, to * layout.width + i))
            else:
                moves.append((g * layout.width + i, g * layout.width + (i ^ 1)))
    return moves


def per_device(stored_tiles, tile_flags, orbitals):
    group_width = lax.axis_size("dev")
    groups = lax.axis_size("grp")
    layout = Layout(group_width)
    order, columns = orbitals.shape
    block = jax.ShapeDtypeStruct((order, columns), F32)
    two = jax.ShapeDtypeStruct((2, order, columns), F32)
    partners = [(i, i ^ 1) for i in range(group_width)]
    semaphore = pltpu.SemaphoreType.DMA

    taken = lax.ppermute(stored_tiles, "dev", partners)[0]
    taken_orbitals = lax.ppermute(orbitals, "dev", partners)
    taken_flags = lax.ppermute(tile_flags, "dev", partners)
    tiles, held = call(
        functools.partial(load_kernel, layout),
        [jax.ShapeDtypeStruct(stored_tiles.shape[1:], F32), block],
        [
            pltpu.with_memory_space_constraint(operand, pltpu.HBM)
            for operand in (tile_flags, stored_tiles[0], orbitals)
        ],
        [HBM] * 3,
        [pltpu.SMEM(tile_flags.shape, jnp.int32), semaphore((3,))],
        flops=10**9,
    )
    mask = call(
        functools.partial(mask_kernel, layout),
        jax.ShapeDtypeStruct((group_width + 1, order), F32),
        [taken_flags],
        flops=10**9,
    )

    *full, made = call(
        functools.partial(send_full_kernel, layout),
        [two] * (layout.rounds + 1),
        [tiles, taken, mask, held, taken_orbitals],
    )
    full_arrived = []
    for r in range(layout.rounds):
        swaps = [
            (i, i ^ (2 * layout.offset(r, i % 2))) for i in range(group_width)
        ]
        full_arrived.append(lax.ppermute(full[r], "dev", swaps))

    last = call(
        functools.partial(send_last_kernel, layout),
        two,
        [tiles, taken, mask, held, taken_orbitals, made],
    )
    last_arrived = lax.ppermute(last, ("grp", "dev"), last_moves(layout, groups))

    odd = call(functools.partial(send_odd_kernel, layout), block, [tiles, held])
    odd_arrived = lax.ppermute(odd, ("grp", "dev"), odd_moves(layout, groups))

    mine, others = call(
        functools.partial(near_kernel, layout),
        [block, block],
        [tiles, held, taken_orbitals],
    )
    others = call(
        functools.partial(full_kernel, layout),
        block,
        [taken, mask, others, *full_arrived],
    )
    others = call(
        functools.partial(back_kernel, layout),
        block,
        [taken, mask, others, last_arrived],
    )
    returned = lax.ppermute(others, "dev", partners)
    mine = call(
        functools.partial(mine_kernel, layout),
        block,
        [tiles, mine, last_arrived, odd_arrived, *full_arrived],
    )
    return mine + returned


def solution(mesh):
    in_specs = (
        P(("grp", "dev"), None, None, None),
        P(("grp", "dev"), None),
        P(("grp", "dev"), None),
    )
    out_specs = P(("grp", "dev"), None)
    return jax.shard_map(
        per_device, mesh=mesh, in_specs=in_specs, out_specs=out_specs, check_vma=False
    )
```

profile of v0, /device:TPU:0, one launch (start us, length us, event | category | flops | bytes accessed | tf_op | source)
XLA Modules:
  0.0 14.9 jit_solution(3864125852150780863)
XLA Ops:
  0.0 0.5 %collective-permute-start.1 = (f32[1,9,128,128]{3,2,1,0:T(8,128)}, f32[1,9,128,128]{3,2,1,0:T(8,128)S(1)}, u32[]{:S(2)}, u32[]{:S(2)}) collective-permute-start(f32[1,9,128,128]{3,2,1,0:T(8,128)} %param.3), channel_id=1, source_target_pairs={{0,1},{1,0},{2,3},{3,2},{4,5},{5,4},{6,7},{7,6},{8,9},{9,8},{10,11... | collective-permute-start | bytes 1769480 | tf_op jit(solution)/shard_map/ppermute | solution.py:300
  0.5 0.1 collective-permute-start.2
  0.5 0.5 %collective-permute-start = (f32[128,256]{1,0:T(8,128)}, f32[128,256]{1,0:T(8,128)S(1)}, u32[]{:S(2)}, u32[]{:S(2)}) collective-permute-start(f32[128,256]{1,0:T(8,128)} %orbitals_in.1), channel_id=1, source_target_pairs={{0,1},{1,0},{2,3},{3,2},{4,5},{5,4},{6,7},{7,6},{8,9},{9,8},{10,11... | collective-permute-start | bytes 393224 | tf_op jit(solution)/shard_map/ppermute | solution.py:301
  1.0 1.2 %shard_map.37 = (f32[9,128,128]{2,1,0:T(8,128)S(1)}, f32[128,256]{1,0:T(8,128)S(1)}) custom-call(s32[1,9]{1,0:T(1,128)} %flags_in.1, f32[9,128,128]{2,1,0:T(8,128)} %bitcast.6, f32[128,256]{1,0:T(8,128)} %orbitals_in.1), custom_call_target="tpu_custom_call" | custom-call | flops 1000000000 | tf_op jit(solution)/shard_map/pallas_call | solution.py:251
  2.1 0.2 %collective-permute-done.2.flags = s32[1,9]{1,0:T(1,128)S(1)} collective-permute-done((s32[1,9]{1,0:T(1,128)}, s32[1,9]{1,0:T(1,128)S(1)}, u32[]{:S(2)}, u32[]{:S(2)}) %collective-permute-start.2) | collective-permute-done | bytes 68 | tf_op jit(solution)/shard_map/ppermute | solution.py:302
  2.3 0.1 shard_map.39.mask
  2.4 0.1 collective-permute-done.taken_orbitals
  2.5 0.0 collective-permute-done.1
  2.5 0.4 %shard_map.40 = (f32[2,128,256]{2,1,0:T(8,128)S(1)}, f32[2,128,256]{2,1,0:T(8,128)S(1)}) custom-call(f32[9,128,128]{2,1,0:T(8,128)S(1)} %get-tuple-element.11.tiles, f32[9,128,128]{2,1,0:T(8,128)S(1)} %bitcast.2, f32[9,128]{1,0:T(8,128)S(1)} %shard_map.39.mask, f32[128,256]{1,0:T(8,128)S(1)} %get-tuple-element.12.orbitals, ...), custom_call_target="tpu_custom_call" | custom-call | tf_op jit(solution)/shard_map/pallas_call | solution.py:251
  2.9 2.6 %collective-permute-start.5 = (f32[2,128,256]{2,1,0:T(8,128)S(1)}, f32[2,128,256]{2,1,0:T(8,128)S(1)}, u32[]{:S(2)}, u32[]{:S(2)}) collective-permute-start(f32[2,128,256]{2,1,0:T(8,128)S(1)} %get-tuple-element.15), channel_id=1, source_target_pairs={{0,2},{1,7},{2,0},{3,5},{4,6},{5,3},{6,4},{7,1},{8,10},{9,15},{10,... | collective-permute-start | bytes 786440 | tf_op jit(solution)/shard_map/ppermute | solution.py:331
  5.5 0.3 %shard_map.41 = f32[2,128,256]{2,1,0:T(8,128)S(1)} custom-call(f32[9,128,128]{2,1,0:T(8,128)S(1)} %get-tuple-element.11.tiles, f32[9,128,128]{2,1,0:T(8,128)S(1)} %bitcast.3, f32[9,128]{1,0:T(8,128)S(1)} %shard_map.39.mask, f32[128,256]{1,0:T(8,128)S(1)} %get-tuple-element.12.orbitals, f32[128,256]{1,0:T(8,128)S(1)} %collective-permute-done.taken_orbitals, ...), custom_call_target="tpu_custom_call" | custom-call | tf_op jit(solution)/shard_map/pallas_call | solution.py:251
  5.8 1.4 %collective-permute-start.3 = (f32[2,128,256]{2,1,0:T(8,128)S(1)}, f32[2,128,256]{2,1,0:T(8,128)S(1)}, u32[]{:S(2)}, u32[]{:S(2)}) collective-permute-start(f32[2,128,256]{2,1,0:T(8,128)S(1)} %shard_map.41), channel_id=1, source_target_pairs={{0,8},{1,5},{2,10},{3,7},{4,12},{5,1},{6,14},{7,3},{8,0},{9,13},{1... | collective-permute-start | bytes 786440 | tf_op jit(solution)/shard_map/ppermute | solution.py:338
  7.2 0.1 collective-permute-start.4
  7.3 0.3 %shard_map.38 = (f32[128,256]{1,0:T(8,128)S(1)}, f32[128,256]{1,0:T(8,128)S(1)}) custom-call(f32[9,128,128]{2,1,0:T(8,128)S(1)} %get-tuple-element.11.tiles, f32[128,256]{1,0:T(8,128)S(1)} %get-tuple-element.12.orbitals, f32[128,256]{1,0:T(8,128)S(1)} %collective-permute-done.taken_orbitals), custom_call_target="tpu_custom_call" | custom-call | tf_op jit(solution)/shard_map/pallas_call | solution.py:251
  7.6 4.5 %collective-permute-done.5.refs_0_ = f32[2,128,256]{2,1,0:T(8,128)S(1)} collective-permute-done((f32[2,128,256]{2,1,0:T(8,128)S(1)}, f32[2,128,256]{2,1,0:T(8,128)S(1)}, u32[]{:S(2)}, u32[]{:S(2)}) %collective-permute-start.5) | collective-permute-done | bytes 262176 | tf_op jit(solution)/shard_map/ppermute | solution.py:331
  12.0 0.2 %shard_map.44.others_in = f32[128,256]{1,0:T(8,128)S(1)} custom-call(f32[9,128,128]{2,1,0:T(8,128)S(1)} %bitcast.4, f32[9,128]{1,0:T(8,128)S(1)} %shard_map.39.mask, f32[128,256]{1,0:T(8,128)S(1)} %get-tuple-element.16.others_in, f32[2,128,256]{2,1,0:T(8,128)S(1)} %collective-permute-done.5.refs_0_), custom_call_target="tpu_custom_call" | custom-call | tf_op jit(solution)/shard_map/pallas_call | solution.py:251
  12.3 0.0 collective-permute-done.3.came
  12.3 0.2 %shard_map.45 = f32[128,256]{1,0:T(8,128)S(1)} custom-call(f32[9,128,128]{2,1,0:T(8,128)S(1)} %bitcast.5, f32[9,128]{1,0:T(8,128)S(1)} %shard_map.39.mask, f32[128,256]{1,0:T(8,128)S(1)} %shard_map.44.others_in, f32[2,128,256]{2,1,0:T(8,128)S(1)} %collective-permute-done.3.came), custom_call_target="tpu_custom_call" | custom-call | tf_op jit(solution)/shard_map/pallas_call | solution.py:251
  12.5 0.7 %collective-permute-start.6 = (f32[128,256]{1,0:T(8,128)S(1)}, f32[128,256]{1,0:T(8,128)S(1)}, u32[]{:S(2)}, u32[]{:S(2)}) collective-permute-start(f32[128,256]{1,0:T(8,128)S(1)} %shard_map.45), channel_id=1, source_target_pairs={{0,1},{1,0},{2,3},{3,2},{4,5},{5,4},{6,7},{7,6},{8,9},{9,8},{10,11... | collective-permute-start | bytes 393224 | tf_op jit(solution)/shard_map/ppermute | solution.py:358
  13.2 0.0 collective-permute-done.4.odd_in
  13.2 0.5 %shard_map.43 = f32[128,256]{1,0:T(8,128)S(1)} custom-call(f32[9,128,128]{2,1,0:T(8,128)S(1)} %get-tuple-element.11.tiles, f32[128,256]{1,0:T(8,128)S(1)} %get-tuple-element.13.mine_in, f32[2,128,256]{2,1,0:T(8,128)S(1)} %collective-permute-done.3.came, f32[128,256]{1,0:T(8,128)S(1)} %collective-permute-done.4.odd_in, ...), custom_call_target="tpu_custom_call" | custom-call | tf_op jit(solution)/shard_map/pallas_call | solution.py:251
  13.7 0.5 %collective-permute-done.6 = f32[128,256]{1,0:T(8,128)S(1)} collective-permute-done((f32[128,256]{1,0:T(8,128)S(1)}, f32[128,256]{1,0:T(8,128)S(1)}, u32[]{:S(2)}, u32[]{:S(2)}) %collective-permute-start.6) | collective-permute-done | bytes 131104 | tf_op jit(solution)/shard_map/ppermute | solution.py:358
  14.2 0.7 %add.3 = f32[128,256]{1,0:T(8,128)} add(f32[128,256]{1,0:T(8,128)S(1)} %shard_map.43, f32[128,256]{1,0:T(8,128)S(1)} %collective-permute-done.6) | non-fusion elementwise | flops 32768 | bytes 393216 | tf_op jit(solution)/shard_map/add | solution.py:364
  (1 shorter events, 0.0 us)
Async XLA Ops:
  0.0 2.5 %collective-permute-start.1 = (f32[1,9,128,128]{3,2,1,0:T(8,128)}, f32[1,9,128,128]{3,2,1,0:T(8,128)S(1)}, u32[]{:S(2)}, u32[]{:S(2)}) collective-permute-start(f32[1,9,128,128]{3,2,1,0:T(8,128)} %param.3), channel_id=1, source_target_pairs={{0,1},{1,0},{2,3},{3,2},{4,5},{5,4},{6,7},{7,6},{8,9},{9,8},{10,11... | collective-permute-start | bytes 1769480 | tf_op jit(solution)/shard_map/ppermute | solution.py:300
  0.5 1.8 %collective-permute-start.2 = (s32[1,9]{1,0:T(1,128)}, s32[1,9]{1,0:T(1,128)S(1)}, u32[]{:S(2)}, u32[]{:S(2)}) collective-permute-start(s32[1,9]{1,0:T(1,128)} %flags_in.1), channel_id=1, source_target_pairs={{0,1},{1,0},{2,3},{3,2},{4,5},{5,4},{6,7},{7,6},{8,9},{9,8},{10,11... | collective-permute-start | bytes 116 | tf_op jit(solution)/shard_map/ppermute | solution.py:302
  0.5 2.0 %collective-permute-start = (f32[128,256]{1,0:T(8,128)}, f32[128,256]{1,0:T(8,128)S(1)}, u32[]{:S(2)}, u32[]{:S(2)}) collective-permute-start(f32[128,256]{1,0:T(8,128)} %orbitals_in.1), channel_id=1, source_target_pairs={{0,1},{1,0},{2,3},{3,2},{4,5},{5,4},{6,7},{7,6},{8,9},{9,8},{10,11... | collective-permute-start | bytes 393224 | tf_op jit(solution)/shard_map/ppermute | solution.py:301
  2.9 9.2 %collective-permute-start.5 = (f32[2,128,256]{2,1,0:T(8,128)S(1)}, f32[2,128,256]{2,1,0:T(8,128)S(1)}, u32[]{:S(2)}, u32[]{:S(2)}) collective-permute-start(f32[2,128,256]{2,1,0:T(8,128)S(1)} %get-tuple-element.15), channel_id=1, source_target_pairs={{0,2},{1,7},{2,0},{3,5},{4,6},{5,3},{6,4},{7,1},{8,10},{9,15},{10,... | collective-permute-start | bytes 786440 | tf_op jit(solution)/shard_map/ppermute | solution.py:331
  5.8 6.5 %collective-permute-start.3 = (f32[2,128,256]{2,1,0:T(8,128)S(1)}, f32[2,128,256]{2,1,0:T(8,128)S(1)}, u32[]{:S(2)}, u32[]{:S(2)}) collective-permute-start(f32[2,128,256]{2,1,0:T(8,128)S(1)} %shard_map.41), channel_id=1, source_target_pairs={{0,8},{1,5},{2,10},{3,7},{4,12},{5,1},{6,14},{7,3},{8,0},{9,13},{1... | collective-permute-start | bytes 786440 | tf_op jit(solution)/shard_map/ppermute | solution.py:338
  7.2 6.0 %collective-permute-start.4 = (f32[128,256]{1,0:T(8,128)S(1)}, f32[128,256]{1,0:T(8,128)S(1)}, u32[]{:S(2)}, u32[]{:S(2)}) collective-permute-start(f32[128,256]{1,0:T(8,128)S(1)} %shard_map.42), channel_id=1, source_target_pairs={{0,1},{1,0},{2,3},{3,2},{4,5},{5,4},{6,7},{7,6},{8,16},{9,17},{10,... | collective-permute-start | bytes 393224 | tf_op jit(solution)/shard_map/ppermute | solution.py:341
  12.5 1.7 %collective-permute-start.6 = (f32[128,256]{1,0:T(8,128)S(1)}, f32[128,256]{1,0:T(8,128)S(1)}, u32[]{:S(2)}, u32[]{:S(2)}) collective-permute-start(f32[128,256]{1,0:T(8,128)S(1)} %shard_map.45), channel_id=1, source_target_pairs={{0,1},{1,0},{2,3},{3,2},{4,5},{5,4},{6,7},{7,6},{8,9},{9,8},{10,11... | collective-permute-start | bytes 393224 | tf_op jit(solution)/shard_map/ppermute | solution.py:358
where the time goes:
time: 15 us; the launch traced here: 14.9 us
  starting transfers between devices  5.68 us (38%)
  waiting for transfers between devices  5.29 us (35%)
  Pallas kernels  3.17 us (21%)
  other arithmetic  0.67 us (4%)
    ppermute x1, waiting for transfers between devices, per_device(): full_arrived.append(lax.ppermute(full[r], 'dev', swaps))  4.48 us
    pallas_call x9, Pallas kernels, call(): pl.pallas_call(body, out_shape=outs, in_specs=specs or [VMEM] * len(opera...  3.17 us
    ppermute x1, starting transfers between devices, per_device(): full_arrived.append(lax.ppermute(full[r], 'dev', swaps))  2.6 us
    ppermute x1, starting transfers between devices, per_device(): lax.ppermute(last, ('grp', 'dev'), last_moves(layout, groups))  1.35 us
    ppermute x1, starting transfers between devices, per_device(): returned = lax.ppermute(others, 'dev', partners)  0.69 us
    add x1, other arithmetic, per_device(): return mine + returned  0.67 us
    ppermute x1, waiting for transfers between devices, per_device(): returned = lax.ppermute(others, 'dev', partners)  0.52 us
    ppermute x1, starting transfers between devices, per_device(): taken_orbitals = lax.ppermute(orbitals, 'dev', partners)  0.45 us
  transfers between devices with their start and end apart: 7, of which 4 were waited for; matrix products, arithmetic and copies ran while one was open for 0% of the time, Pallas kernels for 19%

commit v1 on v0

--- a/solution.py
+++ b/solution.py
@@ -75,17 +75,17 @@
 
 
 def pair_terms(far, tiles, taken, mask, own, other, out):
-    lefts = []
+    dot = functools.partial(
+        lax.dot_general,
+        dimension_numbers=(((0,), (0,)), ((), ())),
+        preferred_element_type=F32,
+    )
+    right_high, right_low = parted(jnp.concatenate([own, other], axis=0))
     for k in range(2):
         slot = 2 * far + k
         stack = jnp.concatenate([tiles[slot], taken_tile(taken, mask, slot)], axis=0)
-        lefts.append(stack.T)
-    terms = times(
-        jnp.concatenate(lefts, axis=0), jnp.concatenate([own, other], axis=0)
-    )
-    order = own.shape[0]
-    out[0] = terms[:order]
-    out[1] = terms[order:]
+        high, low = parted(stack)
+        out[k] = dot(high, right_high) + dot(high, right_low) + dot(low, right_high)
 
 
 def send_full_kernel(layout, tiles, taken, mask, orbitals, taken_orbitals, *outs):

time: 15 us -> 15.1 us (level)
  no operation moved by 1% of the time
where the time goes in v1:
time: 15.1 us; the launch traced here: 14.9 us
  starting transfers between devices  5.72 us (38%)
  waiting for transfers between devices  5.29 us (35%)
  Pallas kernels  3.14 us (21%)
  other arithmetic  0.67 us (4%)
    ppermute x1, waiting for transfers between devices, per_device(): full_arrived.append(lax.ppermute(full[r], 'dev', swaps))  4.48 us
    pallas_call x9, Pallas kernels, call(): pl.pallas_call(body, out_shape=outs, in_specs=specs or [VMEM] * len(opera...  3.14 us
    ppermute x1, starting transfers between devices, per_device(): full_arrived.append(lax.ppermute(full[r], 'dev', swaps))  2.63 us
    ppermute x1, starting transfers between devices, per_device(): lax.ppermute(last, ('grp', 'dev'), last_moves(layout, groups))  1.35 us
    ppermute x1, starting transfers between devices, per_device(): returned = lax.ppermute(others, 'dev', partners)  0.71 us
    add x1, other arithmetic, per_device(): return mine + returned  0.67 us
    ppermute x1, waiting for transfers between devices, per_device(): returned = lax.ppermute(others, 'dev', partners)  0.52 us
    ppermute x1, starting transfers between devices, per_device(): taken = lax.ppermute(stored_tiles, 'dev', partners)[0]  0.45 us
  transfers between devices with their start and end apart: 7, of which 4 were waited for; matrix products, arithmetic and copies ran while one was open for 0% of the time, Pallas kernels for 19%

profile of v1, /device:TPU:0, one launch (start us, length us, event | category | flops | bytes accessed | tf_op | source)
XLA Modules:
  0.0 14.9 jit_solution(16165167330952633537)
XLA Ops:
  0.0 0.5 %collective-permute-start.1 = (f32[1,9,128,128]{3,2,1,0:T(8,128)}, f32[1,9,128,128]{3,2,1,0:T(8,128)S(1)}, u32[]{:S(2)}, u32[]{:S(2)}) collective-permute-start(f32[1,9,128,128]{3,2,1,0:T(8,128)} %param.3), channel_id=1, source_target_pairs={{0,1},{1,0},{2,3},{3,2},{4,5},{5,4},{6,7},{7,6},{8,9},{9,8},{10,11... | collective-permute-start | bytes 1769480 | tf_op jit(solution)/shard_map/ppermute | solution.py:300
  0.5 0.1 collective-permute-start.2
  0.5 0.5 %collective-permute-start = (f32[128,256]{1,0:T(8,128)}, f32[128,256]{1,0:T(8,128)S(1)}, u32[]{:S(2)}, u32[]{:S(2)}) collective-permute-start(f32[128,256]{1,0:T(8,128)} %orbitals_in.1), channel_id=1, source_target_pairs={{0,1},{1,0},{2,3},{3,2},{4,5},{5,4},{6,7},{7,6},{8,9},{9,8},{10,11... | collective-permute-start | bytes 393224 | tf_op jit(solution)/shard_map/ppermute | solution.py:301
  1.0 1.2 %shard_map.37 = (f32[9,128,128]{2,1,0:T(8,128)S(1)}, f32[128,256]{1,0:T(8,128)S(1)}) custom-call(s32[1,9]{1,0:T(1,128)} %flags_in.1, f32[9,128,128]{2,1,0:T(8,128)} %bitcast.6, f32[128,256]{1,0:T(8,128)} %orbitals_in.1), custom_call_target="tpu_custom_call" | custom-call | flops 1000000000 | tf_op jit(solution)/shard_map/pallas_call | solution.py:251
  2.1 0.2 %collective-permute-done.2.flags = s32[1,9]{1,0:T(1,128)S(1)} collective-permute-done((s32[1,9]{1,0:T(1,128)}, s32[1,9]{1,0:T(1,128)S(1)}, u32[]{:S(2)}, u32[]{:S(2)}) %collective-permute-start.2) | collective-permute-done | bytes 68 | tf_op jit(solution)/shard_map/ppermute | solution.py:302
  2.3 0.1 shard_map.39.mask
  2.4 0.1 collective-permute-done.taken_orbitals
  2.5 0.0 collective-permute-done.1
  2.5 0.3 %shard_map.40 = (f32[2,128,256]{2,1,0:T(8,128)S(1)}, f32[2,128,256]{2,1,0:T(8,128)S(1)}) custom-call(f32[9,128,128]{2,1,0:T(8,128)S(1)} %get-tuple-element.11.tiles, f32[9,128,128]{2,1,0:T(8,128)S(1)} %bitcast.2, f32[9,128]{1,0:T(8,128)S(1)} %shard_map.39.mask, f32[128,256]{1,0:T(8,128)S(1)} %get-tuple-element.12.orbitals, ...), custom_call_target="tpu_custom_call" | custom-call | tf_op jit(solution)/shard_map/pallas_call | solution.py:251
  2.8 2.6 %collective-permute-start.5 = (f32[2,128,256]{2,1,0:T(8,128)S(1)}, f32[2,128,256]{2,1,0:T(8,128)S(1)}, u32[]{:S(2)}, u32[]{:S(2)}) collective-permute-start(f32[2,128,256]{2,1,0:T(8,128)S(1)} %get-tuple-element.15), channel_id=1, source_target_pairs={{0,2},{1,7},{2,0},{3,5},{4,6},{5,3},{6,4},{7,1},{8,10},{9,15},{10,... | collective-permute-start | bytes 786440 | tf_op jit(solution)/shard_map/ppermute | solution.py:331
  5.5 0.3 %shard_map.41 = f32[2,128,256]{2,1,0:T(8,128)S(1)} custom-call(f32[9,128,128]{2,1,0:T(8,128)S(1)} %get-tuple-element.11.tiles, f32[9,128,128]{2,1,0:T(8,128)S(1)} %bitcast.3, f32[9,128]{1,0:T(8,128)S(1)} %shard_map.39.mask, f32[128,256]{1,0:T(8,128)S(1)} %get-tuple-element.12.orbitals, f32[128,256]{1,0:T(8,128)S(1)} %collective-permute-done.taken_orbitals, ...), custom_call_target="tpu_custom_call" | custom-call | tf_op jit(solution)/shard_map/pallas_call | solution.py:251
  5.8 1.4 %collective-permute-start.3 = (f32[2,128,256]{2,1,0:T(8,128)S(1)}, f32[2,128,256]{2,1,0:T(8,128)S(1)}, u32[]{:S(2)}, u32[]{:S(2)}) collective-permute-start(f32[2,128,256]{2,1,0:T(8,128)S(1)} %shard_map.41), channel_id=1, source_target_pairs={{0,8},{1,5},{2,10},{3,7},{4,12},{5,1},{6,14},{7,3},{8,0},{9,13},{1... | collective-permute-start | bytes 786440 | tf_op jit(solution)/shard_map/ppermute | solution.py:338
  7.2 0.1 collective-permute-start.4
  7.3 0.3 %shard_map.38 = (f32[128,256]{1,0:T(8,128)S(1)}, f32[128,256]{1,0:T(8,128)S(1)}) custom-call(f32[9,128,128]{2,1,0:T(8,128)S(1)} %get-tuple-element.11.tiles, f32[128,256]{1,0:T(8,128)S(1)} %get-tuple-element.12.orbitals, f32[128,256]{1,0:T(8,128)S(1)} %collective-permute-done.taken_orbitals), custom_call_target="tpu_custom_call" | custom-call | tf_op jit(solution)/shard_map/pallas_call | solution.py:251
  7.6 4.5 %collective-permute-done.5.refs_0_ = f32[2,128,256]{2,1,0:T(8,128)S(1)} collective-permute-done((f32[2,128,256]{2,1,0:T(8,128)S(1)}, f32[2,128,256]{2,1,0:T(8,128)S(1)}, u32[]{:S(2)}, u32[]{:S(2)}) %collective-permute-start.5) | collective-permute-done | bytes 262176 | tf_op jit(solution)/shard_map/ppermute | solution.py:331
  12.0 0.2 %shard_map.44.others_in = f32[128,256]{1,0:T(8,128)S(1)} custom-call(f32[9,128,128]{2,1,0:T(8,128)S(1)} %bitcast.4, f32[9,128]{1,0:T(8,128)S(1)} %shard_map.39.mask, f32[128,256]{1,0:T(8,128)S(1)} %get-tuple-element.16.others_in, f32[2,128,256]{2,1,0:T(8,128)S(1)} %collective-permute-done.5.refs_0_), custom_call_target="tpu_custom_call" | custom-call | tf_op jit(solution)/shard_map/pallas_call | solution.py:251
  12.3 0.0 collective-permute-done.3.came
  12.3 0.2 %shard_map.45 = f32[128,256]{1,0:T(8,128)S(1)} custom-call(f32[9,128,128]{2,1,0:T(8,128)S(1)} %bitcast.5, f32[9,128]{1,0:T(8,128)S(1)} %shard_map.39.mask, f32[128,256]{1,0:T(8,128)S(1)} %shard_map.44.others_in, f32[2,128,256]{2,1,0:T(8,128)S(1)} %collective-permute-done.3.came), custom_call_target="tpu_custom_call" | custom-call | tf_op jit(solution)/shard_map/pallas_call | solution.py:251
  12.5 0.7 %collective-permute-start.6 = (f32[128,256]{1,0:T(8,128)S(1)}, f32[128,256]{1,0:T(8,128)S(1)}, u32[]{:S(2)}, u32[]{:S(2)}) collective-permute-start(f32[128,256]{1,0:T(8,128)S(1)} %shard_map.45), channel_id=1, source_target_pairs={{0,1},{1,0},{2,3},{3,2},{4,5},{5,4},{6,7},{7,6},{8,9},{9,8},{10,11... | collective-permute-start | bytes 393224 | tf_op jit(solution)/shard_map/ppermute | solution.py:358
  13.2 0.0 collective-permute-done.4.odd_in
  13.2 0.5 %shard_map.43 = f32[128,256]{1,0:T(8,128)S(1)} custom-call(f32[9,128,128]{2,1,0:T(8,128)S(1)} %get-tuple-element.11.tiles, f32[128,256]{1,0:T(8,128)S(1)} %get-tuple-element.13.mine_in, f32[2,128,256]{2,1,0:T(8,128)S(1)} %collective-permute-done.3.came, f32[128,256]{1,0:T(8,128)S(1)} %collective-permute-done.4.odd_in, ...), custom_call_target="tpu_custom_call" | custom-call | tf_op jit(solution)/shard_map/pallas_call | solution.py:251
  13.7 0.5 %collective-permute-done.6 = f32[128,256]{1,0:T(8,128)S(1)} collective-permute-done((f32[128,256]{1,0:T(8,128)S(1)}, f32[128,256]{1,0:T(8,128)S(1)}, u32[]{:S(2)}, u32[]{:S(2)}) %collective-permute-start.6) | collective-permute-done | bytes 131104 | tf_op jit(solution)/shard_map/ppermute | solution.py:358
  14.2 0.7 %add.3 = f32[128,256]{1,0:T(8,128)} add(f32[128,256]{1,0:T(8,128)S(1)} %shard_map.43, f32[128,256]{1,0:T(8,128)S(1)} %collective-permute-done.6) | non-fusion elementwise | flops 32768 | bytes 393216 | tf_op jit(solution)/shard_map/add | solution.py:364
  (1 shorter events, 0.0 us)
Async XLA Ops:
  0.0 2.5 %collective-permute-start.1 = (f32[1,9,128,128]{3,2,1,0:T(8,128)}, f32[1,9,128,128]{3,2,1,0:T(8,128)S(1)}, u32[]{:S(2)}, u32[]{:S(2)}) collective-permute-start(f32[1,9,128,128]{3,2,1,0:T(8,128)} %param.3), channel_id=1, source_target_pairs={{0,1},{1,0},{2,3},{3,2},{4,5},{5,4},{6,7},{7,6},{8,9},{9,8},{10,11... | collective-permute-start | bytes 1769480 | tf_op jit(solution)/shard_map/ppermute | solution.py:300
  0.5 1.8 %collective-permute-start.2 = (s32[1,9]{1,0:T(1,128)}, s32[1,9]{1,0:T(1,128)S(1)}, u32[]{:S(2)}, u32[]{:S(2)}) collective-permute-start(s32[1,9]{1,0:T(1,128)} %flags_in.1), channel_id=1, source_target_pairs={{0,1},{1,0},{2,3},{3,2},{4,5},{5,4},{6,7},{7,6},{8,9},{9,8},{10,11... | collective-permute-start | bytes 116 | tf_op jit(solution)/shard_map/ppermute | solution.py:302
  0.5 2.0 %collective-permute-start = (f32[128,256]{1,0:T(8,128)}, f32[128,256]{1,0:T(8,128)S(1)}, u32[]{:S(2)}, u32[]{:S(2)}) collective-permute-start(f32[128,256]{1,0:T(8,128)} %orbitals_in.1), channel_id=1, source_target_pairs={{0,1},{1,0},{2,3},{3,2},{4,5},{5,4},{6,7},{7,6},{8,9},{9,8},{10,11... | collective-permute-start | bytes 393224 | tf_op jit(solution)/shard_map/ppermute | solution.py:301
  2.8 9.2 %collective-permute-start.5 = (f32[2,128,256]{2,1,0:T(8,128)S(1)}, f32[2,128,256]{2,1,0:T(8,128)S(1)}, u32[]{:S(2)}, u32[]{:S(2)}) collective-permute-start(f32[2,128,256]{2,1,0:T(8,128)S(1)} %get-tuple-element.15), channel_id=1, source_target_pairs={{0,2},{1,7},{2,0},{3,5},{4,6},{5,3},{6,4},{7,1},{8,10},{9,15},{10,... | collective-permute-start | bytes 786440 | tf_op jit(solution)/shard_map/ppermute | solution.py:331
  5.8 6.5 %collective-permute-start.3 = (f32[2,128,256]{2,1,0:T(8,128)S(1)}, f32[2,128,256]{2,1,0:T(8,128)S(1)}, u32[]{:S(2)}, u32[]{:S(2)}) collective-permute-start(f32[2,128,256]{2,1,0:T(8,128)S(1)} %shard_map.41), channel_id=1, source_target_pairs={{0,8},{1,5},{2,10},{3,7},{4,12},{5,1},{6,14},{7,3},{8,0},{9,13},{1... | collective-permute-start | bytes 786440 | tf_op jit(solution)/shard_map/ppermute | solution.py:338
  7.2 6.1 %collective-permute-start.4 = (f32[128,256]{1,0:T(8,128)S(1)}, f32[128,256]{1,0:T(8,128)S(1)}, u32[]{:S(2)}, u32[]{:S(2)}) collective-permute-start(f32[128,256]{1,0:T(8,128)S(1)} %shard_map.42), channel_id=1, source_target_pairs={{0,1},{1,0},{2,3},{3,2},{4,5},{5,4},{6,7},{7,6},{8,16},{9,17},{10,... | collective-permute-start | bytes 393224 | tf_op jit(solution)/shard_map/ppermute | solution.py:341
  12.5 1.7 %collective-permute-start.6 = (f32[128,256]{1,0:T(8,128)S(1)}, f32[128,256]{1,0:T(8,128)S(1)}, u32[]{:S(2)}, u32[]{:S(2)}) collective-permute-start(f32[128,256]{1,0:T(8,128)S(1)} %shard_map.45), channel_id=1, source_target_pairs={{0,1},{1,0},{2,3},{3,2},{4,5},{5,4},{6,7},{7,6},{8,9},{9,8},{10,11... | collective-permute-start | bytes 393224 | tf_op jit(solution)/shard_map/ppermute | solution.py:358
